TPU v7x, 32 devices: a whole 2x2x4 slice. The times are simulated.
32 devices in a mesh: row: 4 (over z), col: 8 (over y, x, core).
Axes of the slice: x: 2, y: 2, z: 4, core: 2. Of those that a mesh axis runs over, the one named last changes fastest.
Arguments:
- operator_tiles: bfloat16 [16, 32, 9, 64, 64], P('row', 'col'), may hold values from -0.25 to 0.25
- neighbour_codes: int32 [16, 32, 9], P('row', 'col'), may hold values from 0 to 8, as said below
- live_slots: int32 [16, 32], P('row', 'col'), may hold values from 1 to 9, as said below
- prolong_tiles: bfloat16 [16, 32, 6, 64, 64], P('row', 'col'), may hold values from -0.75 to 0.75
- coarse_blocks: int32 [16, 32, 6], P('row', 'col'), may hold values from 0 to 31, as said below
Outputs:
- coarse_band: float32 [8, 256, 1792], P('col', 'row')
Inputs may be any that keep to these rules, and one draw needn't show every extreme that they name: `neighbour_codes`: A fine block's 9 codes differ; slot 0 holds 4, the block itself. Slots 0 to live_slots - 1 of a fine block are used; some fine block uses all 9. `coarse_blocks`: the 6 coarse blocks of a fine block in slab s differ and lie in slabs s - 1, s, s + 1 (mod 8); the first lies in slab s.
All inputs are finite; a program needn't handle non-finite values.
Results may differ from a plain program's by a relative error of at most 0.0029.
Values may be sent and summed in bfloat16 or wider, within the bound.
A program may use at most 128 MiB of HBM per device.

v0:
```python
import jax
import jax.numpy as jnp
from jax import lax
from jax.sharding import PartitionSpec as P

CB = 4


def padded(value, sides, width):
    for axis, dim in sides:
        size, length = (lax.axis_size(axis), value.shape[dim])
        up = [(i, (i + 1) % size) for i in range(size)]
        down = [(j, i) for i, j in up]
        last = lax.slice_in_dim(value, length - width, length, axis=dim)
        first = lax.slice_in_dim(value, 0, width, axis=dim)
        before = lax.ppermute(last, axis, up)
        after = lax.ppermute(first, axis, down)
        value = jnp.concatenate([before, value, after], axis=dim)
    return value


def from_behind(value, axis, steps):
    count = lax.axis_size(axis)
    pairs = [(source, (source + steps) % count) for source in range(count)]
    return lax.ppermute(value, axis, pairs)


def per_device(operator_tiles, neighbour_codes, live_slots, prolong_tiles, coarse_blocks):
    rows_first, rows_second, slot_count = neighbour_codes.shape
    prolong_width = prolong_tiles.shape[2]
    tile_size = operator_tiles.shape[-1]
    columns = lax.axis_size("col")
    slab_index = lax.axis_index("col")
    window_cols = 5 * CB
    window_rows = 3 * CB
    slab_rows = CB * tile_size
    block_count = rows_first * rows_second
    ext_tiles = padded(prolong_tiles, (("row", 0), ("col", 1)), 1)
    ext_blocks = padded(coarse_blocks, (("row", 0), ("col", 1)), 1)
    col_place = jnp.mod(ext_blocks // CB - slab_index + 2, columns) * CB + ext_blocks % CB
    col_place = col_place.reshape(-1, prolong_width)
    flat_tiles = ext_tiles.reshape(-1, prolong_width, tile_size, tile_size)
    first_index = jnp.arange(rows_first, dtype=jnp.int32)[:, None, None]
    second_index = jnp.arange(rows_second, dtype=jnp.int32)[None, :, None]
    source_index = (
        (first_index + neighbour_codes // 3) * (rows_second + 2)
        + second_index
        + neighbour_codes % 3
    )
    live_mask = jnp.arange(slot_count) < live_slots[..., None]
    masked_tiles = jnp.where(
        live_mask[..., None, None], operator_tiles, jnp.zeros((), operator_tiles.dtype)
    )

    def image_row(operands):
        tiles_row, index_row = operands
        products = jnp.einsum(
            "mkab,mklbc->mklac",
            tiles_row,
            flat_tiles[index_row],
            preferred_element_type=jnp.float32,
        )
        block_ids = jnp.arange(rows_second, dtype=jnp.int32)[:, None, None] * window_cols
        segment_ids = (block_ids + col_place[index_row]).reshape(-1)
        placed = jax.ops.segment_sum(
            products.reshape(-1, tile_size, tile_size),
            segment_ids,
            num_segments=rows_second * window_cols,
        )
        return placed.reshape(rows_second, window_cols, tile_size, tile_size).transpose(0, 2, 1, 3)

    image_panel = lax.map(image_row, (masked_tiles, source_index))
    image_panel = image_panel.reshape(block_count * tile_size, window_cols * tile_size).astype(
        jnp.bfloat16
    )
    row_place = jnp.mod(coarse_blocks // CB - slab_index + 1, columns) * CB + coarse_blocks % CB
    row_hot = (row_place[..., None] == jnp.arange(window_rows)).astype(jnp.bfloat16)
    spread = jnp.einsum(
        "xylba,xylr->xybra", prolong_tiles, row_hot, preferred_element_type=jnp.float32
    ).astype(jnp.bfloat16)
    spread = spread.reshape(block_count * tile_size, 3, slab_rows)
    full_term = jnp.einsum("kst,kc->tsc", spread, image_panel, preferred_element_type=jnp.float32)
    from_next = from_behind(full_term[:, 0], "col", -1)
    from_prev = from_behind(full_term[:, 2], "col", 1)
    combined = jnp.pad(full_term[:, 1], ((0, 0), (slab_rows, slab_rows)))
    combined = combined + jnp.pad(from_next, ((0, 0), (2 * slab_rows, 0)))
    combined = lax.psum_scatter(
        combined + jnp.pad(from_prev, ((0, 0), (0, 2 * slab_rows))),
        "row",
        scatter_dimension=0,
        tiled=True,
    )
    return combined[None]


def solution(mesh):
    in_specs = (
        P("row", "col", None, None, None),
        P("row", "col", None),
        P("row", "col"),
        P("row", "col", None, None, None),
        P("row", "col", None),
    )
    out_specs = P("col", "row", None)
    return jax.shard_map(
        per_device, mesh=mesh, in_specs=in_specs, out_specs=out_specs, check_vma=False
    )
```

profile of v0, /device:TPU:0, one launch (start us, length us, event | category | flops | bytes accessed | tf_op | source)
XLA Modules:
  0.0 331.1 jit_solution(17994325483951187273)
XLA Ops:
  6.5 0.7 fusion.27
  7.2 3.0 collective-permute-start
  10.3 2.0 collective-permute-start.1
  12.3 1.2 fusion.25
  13.5 3.8 %collective-permute-start.5 = (bf16[1,4,6,64,64]{4,3,2,1,0:T(8,128)(2,1)S(1)}, bf16[1,4,6,64,64]{4,3,2,1,0:T(8,128)(2,1)S(1)}, u32[]{:S(2)}, u32[]{:S(2)}) collective-permute-start(bf16[1,4,6,64,64]{4,3,2,1,0:T(8,128)(2,1)S(1)} %get-tuple-element.67), channel_id=1, source_target_pairs={{8,0},{16,8},{24,16},{0,24},{9,1},{17,9},{25,17},{1,25},{10,2},{18... | collective-permute-start | bytes 589832 | tf_op jit(solution)/shard_map/ppermute | solution.py:17
  17.4 0.8 iota_compare_fusion.1
  18.1 0.7 fusion.10
  18.9 3.5 %broadcast_select_fusion = bf16[4,4,9,64,64]{4,3,2,1,0:T(8,128)(2,1)} fusion(bf16[4,4,9,64,64]{4,3,2,1,0:T(8,128)(2,1)} %param.7, pred[4,4,9]{2,1,0:T(4,128)(4,1)S(1)} %iota_compare_fusion.1), kind=kLoop, calls=%fused_computation.15 | loop fusion | flops 589824 | bytes 2359440 | tf_op jit(solution)/shard_map/jit(_where)/select_n | solution.py:51
  22.5 2.6 collective-permute-start.3
  25.2 4.2 %convert_bitcast_fusion = bf16[4,4,64,12,64]{4,3,2,1,0:T(8,128)(2,1)} fusion(bf16[4,4,6,64,64]{4,3,2,1,0:T(8,128)(2,1)S(1)} %copy-done.1, s32[4,4,6]{2,1,0:T(4,128)S(1)} %get-tuple-element.71), kind=kOutput, calls=%fused_computation.12 | convolution fusion | flops 10224768 | bytes 2359680 | tf_op jit(solution)/shard_map/xylba,xylr->xybra/dot_general | solution.py:78
  29.4 7.4 %reshape.109 = bf16[1024,3,256]{2,1,0:T(4,128)(2,1)} reshape(bf16[4,4,64,12,64]{4,3,2,1,0:T(8,128)(2,1)} %convert_bitcast_fusion) | data formatting | bytes 3145728 | tf_op jit(solution)/shard_map/reshape | solution.py:81
  36.8 0.3 constant_dynamic-update-slice_fusion.5
  37.2 1.4 copy-done.2
  38.6 0.1 fusion.24
  38.8 2.6 collective-permute-start.7
  41.6 0.7 copy.27
  42.3 11.8 %collective-permute-done.6 = bf16[6,1,6,64,64]{4,3,2,1,0:T(8,128)(2,1)S(1)} collective-permute-done((bf16[6,1,6,64,64]{4,3,2,1,0:T(8,128)(2,1)S(1)}, bf16[6,1,6,64,64]{4,3,2,1,0:T(8,128)(2,1)S(1)}, u32[]{:S(2)}, u32[]{:S(2)}) %collective-permute-start.6) | collective-permute-done | bytes 294944 | tf_op jit(solution)/shard_map/ppermute | solution.py:16
  54.2 3.5 %pad_maximum_fusion = bf16[6,6,6,64,64]{4,3,2,1,0:T(8,128)(2,1)} fusion(bf16[6,1,6,64,64]{4,3,2,1,0:T(8,128)(2,1)S(1)} %collective-permute-done.7, bf16[6,4,6,64,64]{4,3,2,1,0:T(8,128)(2,1)} %copy-done.2, bf16[6,1,6,64,64]{4,3,2,1,0:T(8,128)(2,1)S(1)} %collective-permute-done.6), kind=kLoop, calls=%fused_computation.14 | loop fusion | flops 1769472 | bytes 3538944 | tf_op jit(solution)/shard_map/concatenate | solution.py:18
  57.7 171.0 %while.10 = (s32[]{:T(128)}, bf16[4,4,64,20,64]{4,2,3,1,0:T(8,128)(2,1)}, s32[4,4,9]{2,1,0:T(4,128)S(1)}, s32[36,6]{1,0:T(8,128)}, bf16[36,6,64,64]{3,2,1,0:T(8,...) while((s32[]{:T(128)}, bf16[4,4,64,20,64]{4,2,3,1,0:T(8,128)(2,1)}, ...), condition=%wide.region_2.3_spmd, body=%wide.region_0.2_spmd.sunk | while | flops 114132296 | bytes 32395752 | solution.py:72
  57.8 3.2 gather_fusion.1
  61.0 5.1 %fusion.35 = f32[4,9,6,64,64]{4,3,2,1,0:T(8,128)} fusion(bf16[4,9,6,64,64]{4,3,2,1,0:T(8,128)(2,1)S(1)} %bitcast.57, bf16[4,4,9,64,64]{4,3,2,1,0:T(8,128)(2,1)} %get-tuple-element.133, s32[]{:T(128)} %get-tuple-element.120), kind=kOutput, calls=%fused_computation.3.clone.1 | convolution fusion | flops 113246208 | bytes 5898752 | tf_op jit(solution)/shard_map/while/body/eval_jaxpr/mkab,mklbc->mklac/dot_general | solution.py:57
  66.1 8.5 %copy.52 = f32[216,64,64]{2,1,0:T(8,128)} copy(f32[216,64,64]{1,2,0:T(8,128)} %bitcast.56) | data formatting | bytes 7077888 | tf_op jit(solution)/shard_map/while/body/eval_jaxpr/reshape | solution.py:66
  74.5 0.6 gather_fusion
  75.4 0.1 copy.51
  75.6 0.3 broadcast.131
  75.9 23.1 %scatter_fusion = f32[80,64,64]{2,1,0:T(8,128)S(1)} fusion(f32[80,64,64]{2,1,0:T(8,128)S(1)} %broadcast.131, s32[216]{0:T(256)S(1)} %reshape.129, f32[216,64,64]{2,1,0:T(8,128)} %copy.52), kind=kCustom, calls=%fused_computation.2.clone.1 | custom fusion | flops 884736 | bytes 10617696 | tf_op jit(solution)/shard_map/while/body/eval_jaxpr/scatter-add | solution.py:65
  99.1 1.4 constant_dynamic-update-slice_fusion.8
  100.5 3.2 gather_fusion.1
  103.8 5.1 %fusion.35 = f32[4,9,6,64,64]{4,3,2,1,0:T(8,128)} fusion(bf16[4,9,6,64,64]{4,3,2,1,0:T(8,128)(2,1)S(1)} %bitcast.57, bf16[4,4,9,64,64]{4,3,2,1,0:T(8,128)(2,1)} %get-tuple-element.133, s32[]{:T(128)} %get-tuple-element.120), kind=kOutput, calls=%fused_computation.3.clone.1 | convolution fusion | flops 113246208 | bytes 5898752 | tf_op jit(solution)/shard_map/while/body/eval_jaxpr/mkab,mklbc->mklac/dot_general | solution.py:57
  108.8 8.5 %copy.52 = f32[216,64,64]{2,1,0:T(8,128)} copy(f32[216,64,64]{1,2,0:T(8,128)} %bitcast.56) | data formatting | bytes 7077888 | tf_op jit(solution)/shard_map/while/body/eval_jaxpr/reshape | solution.py:66
  117.3 0.6 gather_fusion
  118.1 0.1 copy.51
  118.3 0.1 reshape.129
  118.4 0.3 broadcast.131
  118.7 23.1 %scatter_fusion = f32[80,64,64]{2,1,0:T(8,128)S(1)} fusion(f32[80,64,64]{2,1,0:T(8,128)S(1)} %broadcast.131, s32[216]{0:T(256)S(1)} %reshape.129, f32[216,64,64]{2,1,0:T(8,128)} %copy.52), kind=kCustom, calls=%fused_computation.2.clone.1 | custom fusion | flops 884736 | bytes 10617696 | tf_op jit(solution)/shard_map/while/body/eval_jaxpr/scatter-add | solution.py:65
  141.8 1.3 constant_dynamic-update-slice_fusion.8
  143.3 3.2 gather_fusion.1
  146.5 5.1 %fusion.35 = f32[4,9,6,64,64]{4,3,2,1,0:T(8,128)} fusion(bf16[4,9,6,64,64]{4,3,2,1,0:T(8,128)(2,1)S(1)} %bitcast.57, bf16[4,4,9,64,64]{4,3,2,1,0:T(8,128)(2,1)} %get-tuple-element.133, s32[]{:T(128)} %get-tuple-element.120), kind=kOutput, calls=%fused_computation.3.clone.1 | convolution fusion | flops 113246208 | bytes 5898752 | tf_op jit(solution)/shard_map/while/body/eval_jaxpr/mkab,mklbc->mklac/dot_general | solution.py:57
  151.6 8.5 %copy.52 = f32[216,64,64]{2,1,0:T(8,128)} copy(f32[216,64,64]{1,2,0:T(8,128)} %bitcast.56) | data formatting | bytes 7077888 | tf_op jit(solution)/shard_map/while/body/eval_jaxpr/reshape | solution.py:66
  160.1 0.6 gather_fusion
  160.9 0.1 copy.51
  161.1 0.3 broadcast.131
  161.4 23.1 %scatter_fusion = f32[80,64,64]{2,1,0:T(8,128)S(1)} fusion(f32[80,64,64]{2,1,0:T(8,128)S(1)} %broadcast.131, s32[216]{0:T(256)S(1)} %reshape.129, f32[216,64,64]{2,1,0:T(8,128)} %copy.52), kind=kCustom, calls=%fused_computation.2.clone.1 | custom fusion | flops 884736 | bytes 10617696 | tf_op jit(solution)/shard_map/while/body/eval_jaxpr/scatter-add | solution.py:65
  184.6 1.4 constant_dynamic-update-slice_fusion.8
  186.0 3.2 gather_fusion.1
  189.3 5.1 %fusion.35 = f32[4,9,6,64,64]{4,3,2,1,0:T(8,128)} fusion(bf16[4,9,6,64,64]{4,3,2,1,0:T(8,128)(2,1)S(1)} %bitcast.57, bf16[4,4,9,64,64]{4,3,2,1,0:T(8,128)(2,1)} %get-tuple-element.133, s32[]{:T(128)} %get-tuple-element.120), kind=kOutput, calls=%fused_computation.3.clone.1 | convolution fusion | flops 113246208 | bytes 5898752 | tf_op jit(solution)/shard_map/while/body/eval_jaxpr/mkab,mklbc->mklac/dot_general | solution.py:57
  194.4 8.5 %copy.52 = f32[216,64,64]{2,1,0:T(8,128)} copy(f32[216,64,64]{1,2,0:T(8,128)} %bitcast.56) | data formatting | bytes 7077888 | tf_op jit(solution)/shard_map/while/body/eval_jaxpr/reshape | solution.py:66
  202.8 0.6 gather_fusion
  203.6 0.1 copy.51
  203.9 0.3 broadcast.131
  204.2 23.1 %scatter_fusion = f32[80,64,64]{2,1,0:T(8,128)S(1)} fusion(f32[80,64,64]{2,1,0:T(8,128)S(1)} %broadcast.131, s32[216]{0:T(256)S(1)} %reshape.129, f32[216,64,64]{2,1,0:T(8,128)} %copy.52), kind=kCustom, calls=%fused_computation.2.clone.1 | custom fusion | flops 884736 | bytes 10617696 | tf_op jit(solution)/shard_map/while/body/eval_jaxpr/scatter-add | solution.py:65
  227.3 1.4 constant_dynamic-update-slice_fusion.8
  228.7 9.6 %copy.28 = bf16[4,4,64,20,64]{2,1,0,4,3:T(4,128)(2,1)} copy(bf16[4,4,64,20,64]{4,2,3,1,0:T(8,128)(2,1)} %get-tuple-element.37) | data formatting | bytes 5242880 | tf_op jit(solution)/shard_map/convert_element_type | solution.py:73
  238.3 8.2 %reshape.106 = bf16[1024,1280,1]{0,1,2:T(8,128)(2,1)S(1)} reshape(bf16[4,4,64,20,64]{2,1,0,4,3:T(4,128)(2,1)} %copy.28) | data formatting | bytes 5242880 | tf_op jit(solution)/shard_map/convert_element_type | solution.py:73
  246.4 3.8 %convolution_bitcast_fusion = f32[256,3,1280]{0,2,1:T(8,128)S(1)} fusion(bf16[1024,1280,1]{0,1,2:T(8,128)(2,1)S(1)} %reshape.106, bf16[1024,3,256]{2,1,0:T(4,128)(2,1)} %reshape.109), kind=kOutput, calls=%fused_computation.13 | convolution fusion | flops 2013265920 | bytes 8126464 | tf_op jit(solution)/shard_map/kst,kc->tsc/dot_general | solution.py:82
  250.3 0.3 slice_bitcast_fusion.2
  250.5 1.5 collective-permute-start.8
  252.0 28.4 %collective-permute-done.8 = f32[256,1280]{0,1:T(8,128)S(1)} collective-permute-done((f32[256,1280]{0,1:T(8,128)S(1)}, f32[256,1280]{0,1:T(8,128)S(1)}, u32[]{:S(2)}, u32[]{:S(2)}) %collective-permute-start.8) | collective-permute-done | bytes 1310752 | tf_op jit(solution)/shard_map/ppermute | solution.py:25
  280.4 2.7 collective-permute-done.9
  283.1 0.3 pad_add_fusion
  283.4 1.7 copy.41
  285.2 36.7 %reduce-scatter.4.cloned.1.call-done = f32[64,1792]{1,0:T(8,128)} async-done(((f32[256,1792]{1,0:T(8,128)}), f32[64,1792]{1,0:T(8,128)}) %reduce-scatter.4.cloned.1.call-update) | async-done | bytes 458768
  321.9 1.3 copy.42
  323.2 1.1 copy.32
  (68 shorter events, 2.2 us)
Async XLA Ops:
  6.5 315.4 %reduce-scatter.4.cloned.1.call-start = ((), (), s32[]{:S(2)}) async-start(), calls=%async_computation.1 | async-start | bytes 2293760
  7.2 15.1 %collective-permute-start = (s32[1,4,6]{2,1,0:T(4,128)S(1)}, s32[1,4,6]{2,1,0:T(4,128)S(1)}, u32[]{:S(2)}, u32[]{:S(2)}) collective-permute-start(s32[1,4,6]{2,1,0:T(4,128)S(1)} %get-tuple-element.74), channel_id=1, source_target_pairs={{0,8},{8,16},{16,24},{24,0},{1,9},{9,17},{17,25},{25,1},{2,10},{10... | collective-permute-start | bytes 296 | tf_op jit(solution)/shard_map/ppermute | solution.py:16
  10.3 12.2 %collective-permute-start.1 = (s32[1,4,6]{2,1,0:T(4,128)S(1)}, s32[1,4,6]{2,1,0:T(4,128)S(1)}, u32[]{:S(2)}, u32[]{:S(2)}) collective-permute-start(s32[1,4,6]{2,1,0:T(4,128)S(1)} %get-tuple-element.73), channel_id=1, source_target_pairs={{8,0},{16,8},{24,16},{0,24},{9,1},{17,9},{25,17},{1,25},{10,2},{18... | collective-permute-start | bytes 296 | tf_op jit(solution)/shard_map/ppermute | solution.py:17
  13.5 23.3 %collective-permute-start.4 = (bf16[1,4,6,64,64]{4,3,2,1,0:T(8,128)(2,1)S(1)}, bf16[1,4,6,64,64]{4,3,2,1,0:T(8,128)(2,1)S(1)}, u32[]{:S(2)}, u32[]{:S(2)}) collective-permute-start(bf16[1,4,6,64,64]{4,3,2,1,0:T(8,128)(2,1)S(1)} %get-tuple-element.68), channel_id=1, source_target_pairs={{0,8},{8,16},{16,24},{24,0},{1,9},{9,17},{17,25},{25,1},{2,10},{10... | collective-permute-start | bytes 589832 | tf_op jit(solution)/shard_map/ppermute | solution.py:16
  13.5 23.6 %collective-permute-start.5 = (bf16[1,4,6,64,64]{4,3,2,1,0:T(8,128)(2,1)S(1)}, bf16[1,4,6,64,64]{4,3,2,1,0:T(8,128)(2,1)S(1)}, u32[]{:S(2)}, u32[]{:S(2)}) collective-permute-start(bf16[1,4,6,64,64]{4,3,2,1,0:T(8,128)(2,1)S(1)} %get-tuple-element.67), channel_id=1, source_target_pairs={{8,0},{16,8},{24,16},{0,24},{9,1},{17,9},{25,17},{1,25},{10,2},{18... | collective-permute-start | bytes 589832 | tf_op jit(solution)/shard_map/ppermute | solution.py:17
  18.8 3.5 %copy-start.3 = (s32[4,4,6]{2,1,0:T(4,128)S(1)}, s32[4,4,6]{2,1,0:T(4,128)}, u32[]{:S(2)}) copy-start(s32[4,4,6]{2,1,0:T(4,128)} %param.11) | copy-start | bytes 1156
  18.8 6.3 %copy-start.1 = (bf16[4,4,6,64,64]{4,3,2,1,0:T(8,128)(2,1)S(1)}, bf16[4,4,6,64,64]{4,3,2,1,0:T(8,128)(2,1)}, u32[]{:S(2)}) copy-start(bf16[4,4,6,64,64]{4,3,2,1,0:T(8,128)(2,1)} %param.10) | copy-start | bytes 2359300
  22.5 19.0 %collective-permute-start.2 = (s32[6,1,6]{2,1,0:T(1,128)S(1)}, s32[6,1,6]{2,1,0:T(1,128)S(1)}, u32[]{:S(2)}, u32[]{:S(2)}) collective-permute-start(s32[6,1,6]{2,1,0:T(1,128)S(1)} %get-tuple-element.69), channel_id=1, source_target_pairs={{0,1},{1,2},{2,3},{3,4},{4,5},{5,6},{6,7},{7,0},{8,9},{9,10},{10,1... | collective-permute-start | bytes 440 | tf_op jit(solution)/shard_map/ppermute | solution.py:16
  22.5 18.9 %collective-permute-start.3 = (s32[6,1,6]{2,1,0:T(1,128)S(1)}, s32[6,1,6]{2,1,0:T(1,128)S(1)}, u32[]{:S(2)}, u32[]{:S(2)}) collective-permute-start(s32[6,1,6]{2,1,0:T(1,128)S(1)} %get-tuple-element.70), channel_id=1, source_target_pairs={{1,0},{2,1},{3,2},{4,3},{5,4},{6,5},{7,6},{0,7},{9,8},{10,9},{11,1... | collective-permute-start | bytes 440 | tf_op jit(solution)/shard_map/ppermute | solution.py:17
  37.2 1.4 copy-start.2
  38.8 15.4 %collective-permute-start.6 = (bf16[6,1,6,64,64]{4,3,2,1,0:T(8,128)(2,1)S(1)}, bf16[6,1,6,64,64]{4,3,2,1,0:T(8,128)(2,1)S(1)}, u32[]{:S(2)}, u32[]{:S(2)}) collective-permute-start(bf16[6,1,6,64,64]{4,3,2,1,0:T(8,128)(2,1)S(1)} %get-tuple-element.65), channel_id=1, source_target_pairs={{0,1},{1,2},{2,3},{3,4},{4,5},{5,6},{6,7},{7,0},{8,9},{9,10},{10,1... | collective-permute-start | bytes 884744 | tf_op jit(solution)/shard_map/ppermute | solution.py:16
  38.8 15.3 %collective-permute-start.7 = (bf16[6,1,6,64,64]{4,3,2,1,0:T(8,128)(2,1)S(1)}, bf16[6,1,6,64,64]{4,3,2,1,0:T(8,128)(2,1)S(1)}, u32[]{:S(2)}, u32[]{:S(2)}) collective-permute-start(bf16[6,1,6,64,64]{4,3,2,1,0:T(8,128)(2,1)S(1)} %get-tuple-element.66), channel_id=1, source_target_pairs={{1,0},{2,1},{3,2},{4,3},{5,4},{6,5},{7,6},{0,7},{9,8},{10,9},{11,1... | collective-permute-start | bytes 884744 | tf_op jit(solution)/shard_map/ppermute | solution.py:17
  66.1 8.5 %copy-start = (s32[36,6]{1,0:T(8,128)S(1)}, s32[36,6]{1,0:T(8,128)}, u32[]{:S(2)}) copy-start(s32[36,6]{1,0:T(8,128)} %get-tuple-element.131) | copy-start | bytes 2596 | tf_op jit(solution)/shard_map/while
  108.8 8.5 %copy-start = (s32[36,6]{1,0:T(8,128)S(1)}, s32[36,6]{1,0:T(8,128)}, u32[]{:S(2)}) copy-start(s32[36,6]{1,0:T(8,128)} %get-tuple-element.131) | copy-start | bytes 2596 | tf_op jit(solution)/shard_map/while
  151.6 8.5 %copy-start = (s32[36,6]{1,0:T(8,128)S(1)}, s32[36,6]{1,0:T(8,128)}, u32[]{:S(2)}) copy-start(s32[36,6]{1,0:T(8,128)} %get-tuple-element.131) | copy-start | bytes 2596 | tf_op jit(solution)/shard_map/while
  194.4 8.5 %copy-start = (s32[36,6]{1,0:T(8,128)S(1)}, s32[36,6]{1,0:T(8,128)}, u32[]{:S(2)}) copy-start(s32[36,6]{1,0:T(8,128)} %get-tuple-element.131) | copy-start | bytes 2596 | tf_op jit(solution)/shard_map/while
  250.5 29.9 %collective-permute-start.8 = (f32[256,1280]{0,1:T(8,128)S(1)}, f32[256,1280]{0,1:T(8,128)S(1)}, u32[]{:S(2)}, u32[]{:S(2)}) collective-permute-start(f32[256,1280]{0,1:T(8,128)S(1)} %get-tuple-element.64), channel_id=1, source_target_pairs={{0,7},{1,0},{2,1},{3,2},{4,3},{5,4},{6,5},{7,6},{8,15},{9,8},{10,9... | collective-permute-start | bytes 3932168 | tf_op jit(solution)/shard_map/ppermute | solution.py:25
  252.0 31.1 %collective-permute-start.9 = (f32[256,1280]{0,1:T(8,128)S(1)}, f32[256,1280]{0,1:T(8,128)S(1)}, u32[]{:S(2)}, u32[]{:S(2)}) collective-permute-start(f32[256,1280]{0,1:T(8,128)S(1)} %get-tuple-element.63), channel_id=1, source_target_pairs={{0,1},{1,2},{2,3},{3,4},{4,5},{5,6},{6,7},{7,0},{8,9},{9,10},{10,1... | collective-permute-start | bytes 3932168 | tf_op jit(solution)/shard_map/ppermute | solution.py:25
Sparse Core Ops, SparseCore 0:
  285.3 36.5 reduce-scatter.3
where the time goes:
time: 335 us; the launch traced here: 331 us
  other arithmetic  102 us (30%)
  local copies, waits for them, and re-layouts  91.8 us (27%)
  waiting for transfers between devices  79.7 us (24%)
  matrix products  28.3 us (8%)
  starting transfers between devices  15.8 us (5%)
  between operations  13.6 us (4%)
    scatter-add x4, other arithmetic, image_row(): jax.ops.segment_sum(products.reshape(-1, tile_size, tile_size), segment_i...  92.6 us
    unnamed x2, waiting for transfers between devices  36.8 us
    reshape x4, local copies, waits for them, and re-layouts, image_row(): products.reshape(-1, tile_size, tile_size)  33.9 us
    ppermute x2, waiting for transfers between devices, from_behind(): return lax.ppermute(value, axis, pairs)  31.1 us
    dot_general x4, matrix products, image_row(): jnp.einsum('mkab,mklbc->mklac', tiles_row, flat_tiles[index_row], preferr...  20.3 us
    convert_element_type x2, local copies, waits for them, and re-layouts, per_device(): image_panel.reshape(block_count * tile_size, window_cols * tile_size)  17.7 us
    gather x4, local copies, waits for them, and re-layouts, image_row(): flat_tiles[index_row]  12.9 us
    ppermute x4, waiting for transfers between devices, padded(): before = lax.ppermute(last, axis, up)  11.8 us
  transfers between devices with their start and end apart: 11, of which 4 were waited for; matrix products, arithmetic and copies ran while one was open for 6% of the time, Pallas kernels for 0%

commit v1 on v0

v1 whole, which is shorter than its diff:
```python
import functools

import jax
import jax.numpy as jnp
from jax import lax
from jax.experimental import pallas as pl
from jax.experimental.pallas import tpu as pltpu
from jax.sharding import PartitionSpec as P

CB = 4
MESH = pl.DeviceIdType.MESH
STRIDE = 16


def kernel(
    dims, n_row, n_col, a_ref, p_ref, ainv_ref, codes_smem, codes_ref, out_ref,
    pext, cext, csm, p2, wc, wl, wr, wt, ac, al, ar, acc, img,
    csend, crecv, own, zsend, zrecv,
    psend_sem, precv_sem, ksend_sem, krecv_sem, copy_sem,
    csend_sem, crecv_sem, zsend_sem, zrecv_sem,
):
    fx, fy, ka, kp, b = dims
    win = 3 * CB
    slab = CB * b
    rows = slab // n_row
    wide = 5 * slab
    me_r, me_c = lax.axis_index("row"), lax.axis_index("col")

    def device(dr, dc):
        return (lax.rem(me_r + dr + n_row, n_row), lax.rem(me_c + dc + n_col, n_col))

    around = [(i, j) for i in (-1, 0, 1) for j in (-1, 0, 1) if (i, j) != (0, 0)]
    partners = {(i % n_row, j % n_col) for i, j in around} | {(k, 0) for k in range(1, n_row)}
    barrier = pltpu.get_barrier_semaphore()
    for i, j in sorted(partners):
        pl.semaphore_signal(barrier, inc=1, device_id=device(i, j), device_id_type=MESH)

    def pack(n, carry):
        x, y = n // fy, n % fy
        for j in range(0, kp, 2):
            pair = [p_ref[n * kp + j], p_ref[n * kp + j + 1]]
            pext[x + 1, y + 1, :, j * b:(j + 2) * b] = jnp.concatenate(pair, axis=1)
        return carry

    lax.fori_loop(0, fx * fy, pack, 0)
    pl.semaphore_wait(barrier, len(partners))

    halo = []
    for t, (i, j) in enumerate(around):
        xs = {-1: 1, 0: pl.ds(1, fx), 1: fx}[i]
        ys = {-1: 1, 0: pl.ds(1, fy), 1: fy}[j]
        xd = {-1: fx + 1, 0: pl.ds(1, fx), 1: 0}[i]
        yd = {-1: fy + 1, 0: pl.ds(1, fy), 1: 0}[j]
        numbers = pltpu.make_async_remote_copy(
            src_ref=codes_ref, dst_ref=cext.at[(1 - i) * 3 + 1 - j],
            send_sem=ksend_sem.at[t], recv_sem=krecv_sem.at[t],
            device_id=device(i, j), device_id_type=MESH,
        )
        tiles = pltpu.make_async_remote_copy(
            src_ref=pext.at[xs, ys], dst_ref=pext.at[xd, yd],
            send_sem=psend_sem.at[t], recv_sem=precv_sem.at[t],
            device_id=device(i, j), device_id_type=MESH,
        )
        halo += [numbers, tiles]
    for copy in halo:
        copy.start()

    lane = lax.broadcasted_iota(jnp.int32, (b, 2 * b), 1)
    lower = lane < b

    def spread(xe, ye, n, read, dst, at):
        e = xe * (fy + 2) + ye
        p2[e, kp] = jnp.zeros((b, 2 * b), p2.dtype)
        for j in range(0, kp, 2):
            pair = pext[xe, ye, :, j * b:(j + 2) * b]
            for h in range(2):
                tile = pair[:, h * b:(h + 1) * b]
                p2[e, j + h] = jnp.concatenate([tile, tile], axis=1)
        for w in range(0, win, 2):
            flat = n * STRIDE + w
            first, second = read(flat), read(flat + 1)
            dst(at, w * b, jnp.where(lower, p2[e, first], p2[e, second]))

    def to_centre(at, c, value):
        wc[at[0], pl.ds(at[1], b), c:c + 2 * b] = value

    def to_left(at, c, value):
        wl[pl.ds(at, b), c:c + 2 * b] = value

    def to_right(at, c, value):
        wr[pl.ds(at, b), c:c + 2 * b] = value

    def read_own(flat):
        return codes_smem[flat // 128, flat % 128]

    def read_near(slot):
        return lambda flat: csm[slot, flat // 128, flat % 128]

    def own_spread(n, carry):
        x, y = n // fy, n % fy
        spread(x + 1, y + 1, n, read_own, to_centre, (x + 1, pl.multiple_of(y * b, b)))
        return carry

    lax.fori_loop(0, fx * fy, own_spread, 0)

    def operator_tile(m, d):
        k = ainv_ref[m * 9 + d]
        tile = a_ref[m * ka + jnp.minimum(k, ka - 1)]
        return jnp.where(jnp.full(tile.shape, k) < ka, tile, jnp.zeros_like(tile))

    zero_tile = jnp.zeros((b, b), a_ref.dtype)

    def bands(x, carry):
        for dx in range(3):
            for y in range(fy):
                for yp in range(0, fy, 2):
                    pair = [
                        operator_tile(x * fy + y, dx * 3 + yy - y + 1) if abs(yy - y) < 2 else zero_tile
                        for yy in (yp, yp + 1)
                    ]
                    ac[x * 3 + dx, y * b:(y + 1) * b, yp * b:(yp + 2) * b] = jnp.concatenate(pair, axis=1)
        return carry

    lax.fori_loop(0, fx, bands, 0)
    for x in range(fx):
        for side, y, dy in ((al, 0, 0), (ar, fy - 1, 2)):
            for xe in range(0, fx + 2, 2):
                pair = [
                    operator_tile(x * fy + y, (xx - x) * 3 + dy) if 0 <= xx - x <= 2 else zero_tile
                    for xx in (xe, xe + 1)
                ]
                side[x * b:(x + 1) * b, xe * b:(xe + 2) * b] = jnp.concatenate(pair, axis=1)

    def own_transposed(x, carry):
        for c in range(3):
            wt[c * slab:(c + 1) * slab, pl.ds(pl.multiple_of(x * fy * b, fy * b), fy * b)] = (
                wc[x + 1, :, c * slab:(c + 1) * slab].T
            )
        return carry

    lax.fori_loop(0, fx, own_transposed, 0)

    for x in range(fx):
        acc[x, :, 0:slab] = jnp.zeros((fy * b, slab), jnp.float32)
        acc[x, :, 4 * slab:] = jnp.zeros((fy * b, slab), jnp.float32)
        total = None
        for dx in range(3):
            if 1 <= x + dx <= fx:
                term = jnp.dot(ac[x * 3 + dx], wc[x + dx], preferred_element_type=jnp.float32)
                total = term if total is None else total + term
        acc[x, :, slab:4 * slab] = total

    for copy in halo:
        copy.wait_recv()
    numbers_in = pltpu.make_async_copy(cext, csm, copy_sem)
    numbers_in.start()
    numbers_in.wait()

    def edge_rows(y, carry):
        at = pl.multiple_of(y * b, b)
        spread(0, y + 1, (fx - 1) * fy + y, read_near(1), to_centre, (0, at))
        spread(fx + 1, y + 1, y, read_near(7), to_centre, (fx + 1, at))
        return carry

    lax.fori_loop(0, fy, edge_rows, 0)

    def edge_columns(x, carry):
        at = pl.multiple_of((x + 1) * b, b)
        spread(x + 1, 0, x * fy + fy - 1, read_near(3), to_left, at)
        spread(x + 1, fy + 1, x * fy, read_near(5), to_right, at)
        return carry

    lax.fori_loop(0, fx, edge_columns, 0)
    spread(0, 0, fx * fy - 1, read_near(0), to_left, 0)
    spread(0, fy + 1, (fx - 1) * fy, read_near(2), to_right, 0)
    spread(fx + 1, 0, fy - 1, read_near(6), to_left, (fx + 1) * b)
    spread(fx + 1, fy + 1, 0, read_near(8), to_right, (fx + 1) * b)

    acc[0, :, slab:4 * slab] += jnp.dot(ac[0], wc[0], preferred_element_type=jnp.float32)
    acc[fx - 1, :, slab:4 * slab] += jnp.dot(
        ac[(fx - 1) * 3 + 2], wc[fx + 1], preferred_element_type=jnp.float32
    )
    left = jnp.dot(al[...], wl[...], preferred_element_type=jnp.float32)
    for x in range(fx):
        acc[x, 0:b, 0:3 * slab] += left[x * b:(x + 1) * b]
    right = jnp.dot(ar[...], wr[...], preferred_element_type=jnp.float32)
    for x in range(fx):
        acc[x, (fy - 1) * b:, 2 * slab:] += right[x * b:(x + 1) * b]
    for x in range(fx):
        img[x * fy * b:(x + 1) * fy * b, :] = acc[x].astype(img.dtype)

    order = [*range(1, n_row), 0]
    across = []
    for side, part, step in ((0, 0, -1), (1, 2, 1)):
        for c in range(5):
            piece = jnp.dot(
                wt[part * slab:(part + 1) * slab, :], img[:, c * slab:(c + 1) * slab],
                preferred_element_type=jnp.float32,
            ).astype(csend.dtype)
            csend[side, :, c * slab:(c + 1) * slab] = piece
        for k in order:
            t = pl.multiple_of(lax.rem(me_r + k, n_row) * rows, rows)
            copy = pltpu.make_async_remote_copy(
                src_ref=csend.at[side, pl.ds(t, rows)], dst_ref=crecv.at[side, pl.ds(t, rows)],
                send_sem=csend_sem.at[side, k], recv_sem=crecv_sem.at[side, k],
                device_id=device(0, step), device_id_type=MESH,
            )
            copy.start()
            across.append((k, copy))
    for c in range(5):
        own[:, c * slab:(c + 1) * slab] = jnp.dot(
            wt[slab:2 * slab, :], img[:, c * slab:(c + 1) * slab], preferred_element_type=jnp.float32
        )

    def combined(t):
        mine = own[pl.ds(t, rows), :]
        from_next = crecv[0, pl.ds(t, rows), :].astype(jnp.float32)
        from_prev = crecv[1, pl.ds(t, rows), :].astype(jnp.float32)
        parts = []
        for c in range(7):
            terms = [
                value[:, (c - shift) * slab:(c - shift + 1) * slab]
                for value, shift in ((mine, 1), (from_next, 2), (from_prev, 0))
                if 0 <= c - shift < 5
            ]
            parts.append(functools.reduce(jnp.add, terms))
        return parts

    down = []
    for k in order:
        for other, copy in across:
            if other == k:
                copy.wait_recv()
        t = pl.multiple_of(lax.rem(me_r + k, n_row) * rows, rows)
        for c, value in enumerate(combined(t)):
            if k:
                zsend[k, :, c * slab:(c + 1) * slab] = value.astype(zsend.dtype)
            else:
                out_ref[:, c * slab:(c + 1) * slab] = value
        if k:
            copy = pltpu.make_async_remote_copy(
                src_ref=zsend.at[k], dst_ref=zrecv.at[k],
                send_sem=zsend_sem.at[k], recv_sem=zrecv_sem.at[k],
                device_id=device(k, 0), device_id_type=MESH,
            )
            copy.start()
            down.append((k, copy))
    for k, copy in down:
        copy.wait_recv()
        out_ref[...] += zrecv[k].astype(jnp.float32)
    for copy in halo:
        copy.wait_send()
    for _, copy in across + down:
        copy.wait_send()


def per_device(operator_tiles, neighbour_codes, live_slots, prolong_tiles, coarse_blocks):
    fx, fy, ka = neighbour_codes.shape
    kp = prolong_tiles.shape[2]
    b = operator_tiles.shape[-1]
    n_row, n_col = lax.axis_size("row"), lax.axis_size("col")
    slab_index = lax.axis_index("col")
    win = 3 * CB
    slab = CB * b
    rows = slab // n_row
    band = 7 * slab
    blocks = fx * fy
    slots = jnp.arange(ka, dtype=jnp.int32)[:, None]
    match = (neighbour_codes[..., None] == jnp.arange(9, dtype=jnp.int32)) & (slots < live_slots[..., None, None])
    ainv = jnp.min(jnp.where(match, slots, ka), axis=2).reshape(-1)
    place = jnp.mod(coarse_blocks // CB - slab_index + 1, n_col) * CB + coarse_blocks % CB
    tiles = jnp.arange(kp, dtype=jnp.int32)[:, None]
    hit = place[..., None] == jnp.arange(STRIDE, dtype=jnp.int32)
    pinv = jnp.min(jnp.where(hit, tiles, kp), axis=2).reshape(-1, 128)
    codes = jnp.pad(pinv, ((0, -pinv.shape[0] % 8), (0, 0)))
    bf, f32 = jnp.bfloat16, jnp.float32
    dma = pltpu.SemaphoreType.DMA
    vmem = pl.BlockSpec(memory_space=pltpu.VMEM)
    smem = pl.BlockSpec(memory_space=pltpu.SMEM)
    out = pl.pallas_call(
        functools.partial(kernel, (fx, fy, ka, kp, b), n_row, n_col),
        out_shape=jax.ShapeDtypeStruct((rows, band), f32),
        in_specs=[vmem, vmem, smem, smem, vmem],
        out_specs=vmem,
        scratch_shapes=[
            pltpu.VMEM((fx + 2, fy + 2, b, kp * b), bf),
            pltpu.VMEM((9, *codes.shape), jnp.int32),
            pltpu.SMEM((9, *codes.shape), jnp.int32),
            pltpu.VMEM(((fx + 2) * (fy + 2), kp + 1, b, 2 * b), bf),
            pltpu.VMEM((fx + 2, fy * b, win * b), bf),
            pltpu.VMEM(((fx + 2) * b, win * b), bf),
            pltpu.VMEM(((fx + 2) * b, win * b), bf),
            pltpu.VMEM((win * b, blocks * b), bf),
            pltpu.VMEM((fx * 3, fy * b, fy * b), bf),
            pltpu.VMEM((fx * b, (fx + 2) * b), bf),
            pltpu.VMEM((fx * b, (fx + 2) * b), bf),
            pltpu.VMEM((fx, fy * b, 5 * slab), f32),
            pltpu.VMEM((blocks * b, 5 * slab), bf),
            pltpu.VMEM((2, slab, 5 * slab), bf),
            pltpu.VMEM((2, slab, 5 * slab), bf),
            pltpu.VMEM((slab, 5 * slab), f32),
            pltpu.VMEM((n_row, rows, band), bf),
            pltpu.VMEM((n_row, rows, band), bf),
            dma((8,)), dma((8,)), dma((8,)), dma((8,)), dma,
            dma((2, n_row)), dma((2, n_row)), dma((n_row,)), dma((n_row,)),
        ],
        compiler_params=pltpu.CompilerParams(
            collective_id=0, has_side_effects=True, vmem_limit_bytes=50 * 1024 * 1024
        ),
    )(
        operator_tiles.reshape(-1, b, b), prolong_tiles.reshape(-1, b, b), ainv, codes, codes,
    )
    return out[None]


def solution(mesh):
    in_specs = (
        P("row", "col", None, None, None),
        P("row", "col", None),
        P("row", "col"),
        P("row", "col", None, None, None),
        P("row", "col", None),
    )
    out_specs = P("col", "row", None)
    return jax.shard_map(
        per_device, mesh=mesh, in_specs=in_specs, out_specs=out_specs, check_vma=False
    )
```

time: 335 us -> 59.6 us (0.18)
  the two profiles are of different devices: /device:TPU:0 before, /device:TPU:11 now
where the time goes in v1:
time: 59.6 us; the launch traced here: 59.3 us
  Pallas kernels  54.3 us (91%)
  local copies, waits for them, and re-layouts  3.28 us (6%)
  other arithmetic  1.67 us (3%)
    pallas_call x1, Pallas kernels, per_device(): pl.pallas_call(functools.partial(kernel, (fx, fy, ka, kp, b), n_row, n_co...  54.3 us
    unnamed x4, local copies, waits for them, and re-layouts  2.98 us

profile of v1, /device:TPU:11, one launch (start us, length us, event | category | flops | bytes accessed | tf_op | source)
XLA Modules:
  0.0 59.3 jit_solution(5460381006747789502)
XLA Ops:
  0.0 0.7 %fusion.5 = s32[4,4,6]{2,1,0:T(4,128)S(1)} fusion(s32[4,4,6]{2,1,0:T(4,128)} %param.9, s32[]{:T(128)S(6)} %axis_index.12), kind=kLoop, calls=%fused_computation.18 | loop fusion | flops 3264 | bytes 772 | tf_op jit(solution)/shard_map/add | solution.py:271
  0.7 0.1 copy.7
  0.8 0.1 select_reduce_fusion.1
  0.9 0.1 reshape.25
  1.0 0.7 %iota_compare_fusion.2 = pred[4,4,9]{1,2,0:T(8,128)(4,1)S(1)} fusion(s32[4,4]{1,0:T(4,128)} %param.7), kind=kLoop, calls=%fused_computation.5 | loop fusion | flops 144 | bytes 208 | tf_op jit(solution)/shard_map/lt | solution.py:269
  1.7 0.8 %copy.6 = s32[4,4,9]{1,2,0:T(8,128)S(1)} copy(s32[4,4,9]{2,1,0:T(4,128)} %param.6) | data formatting | bytes 1152 | tf_op args[1]
  2.5 0.1 select_reduce_fusion
  2.7 0.1 reshape.24.ainv_ref
  2.8 0.0 copy-start
  2.8 1.4 %copy-done = bf16[4,4,6,64,64]{4,3,2,1,0:T(8,128)(2,1)S(1)} copy-done((bf16[4,4,6,64,64]{4,3,2,1,0:T(8,128)(2,1)S(1)}, bf16[4,4,6,64,64]{4,3,2,1,0:T(8,128)(2,1)}, u32[]{:S(2)}) %copy-start) | copy-done | bytes 786456
  4.2 54.3 %shard_map.55 = f32[64,1792]{1,0:T(8,128)S(1)} custom-call(bf16[144,64,64]{2,1,0:T(8,128)(2,1)} %bitcast.5, bf16[96,64,64]{2,1,0:T(8,128)(2,1)S(1)} %bitcast.4, s32[144]{0:T(256)S(1)} %reshape.24.ainv_ref, s32[8,128]{1,0:T(8,128)S(1)} %pad.4.codes_smem.codes_ref, s32[8,128]{1,0:T(8,128)S(1)} %pad.4.codes_smem.codes_ref), custom_call_target="tpu_custom_call" | custom-call | tf_op jit(solution)/shard_map/pallas_call | solution.py:280
  58.5 0.8 %copy.9 = f32[1,64,1792]{2,1,0:T(8,128)} copy(f32[1,64,1792]{2,1,0:T(8,128)S(1)} %bitcast.3) | data formatting | bytes 917504
  (1 shorter events, 0.0 us)
Async XLA Ops:
  2.8 1.4 %copy-start = (bf16[4,4,6,64,64]{4,3,2,1,0:T(8,128)(2,1)S(1)}, bf16[4,4,6,64,64]{4,3,2,1,0:T(8,128)(2,1)}, u32[]{:S(2)}) copy-start(bf16[4,4,6,64,64]{4,3,2,1,0:T(8,128)(2,1)} %param.8) | copy-start | bytes 2359300

commit v2 on v1

--- a/solution.py
+++ b/solution.py
@@ -13,10 +13,10 @@
 
 
 def kernel(
-    dims, n_row, n_col, a_ref, p_ref, ainv_ref, codes_smem, codes_ref, out_ref,
-    pext, cext, csm, p2, wc, wl, wr, wt, ac, al, ar, acc, img,
+    dims, n_row, n_col, a_hbm, p_hbm, ainv_ref, codes_smem, codes_ref, out_ref,
+    a_ref, p_ref, pext, cext, csm, p2, wc, wl, wr, wt, ac, al, ar, acc, img,
     csend, crecv, own, zsend, zrecv,
-    psend_sem, precv_sem, ksend_sem, krecv_sem, copy_sem,
+    psend_sem, precv_sem, ksend_sem, krecv_sem, copy_sem, a_sem, p_sem,
     csend_sem, crecv_sem, zsend_sem, zrecv_sem,
 ):
     fx, fy, ka, kp, b = dims
@@ -26,6 +26,11 @@
     wide = 5 * slab
     me_r, me_c = lax.axis_index("row"), lax.axis_index("col")
 
+    tiles_in = pltpu.make_async_copy(p_hbm, p_ref, p_sem)
+    tiles_in.start()
+    operator_in = pltpu.make_async_copy(a_hbm, a_ref, a_sem)
+    operator_in.start()
+
     def device(dr, dc):
         return (lax.rem(me_r + dr + n_row, n_row), lax.rem(me_c + dc + n_col, n_col))
 
@@ -42,6 +47,7 @@
             pext[x + 1, y + 1, :, j * b:(j + 2) * b] = jnp.concatenate(pair, axis=1)
         return carry
 
+    tiles_in.wait()
     lax.fori_loop(0, fx * fy, pack, 0)
     pl.semaphore_wait(barrier, len(partners))
 
@@ -109,6 +115,7 @@
         return jnp.where(jnp.full(tile.shape, k) < ka, tile, jnp.zeros_like(tile))
 
     zero_tile = jnp.zeros((b, b), a_ref.dtype)
+    operator_in.wait()
 
     def bands(x, carry):
         for dx in range(3):
@@ -189,7 +196,12 @@
     for x in range(fx):
         img[x * fy * b:(x + 1) * fy * b, :] = acc[x].astype(img.dtype)
 
-    order = [*range(1, n_row), 0]
+    relayed = n_row == 4
+    if relayed:
+        far = jnp.where(2 * me_r < n_row, 3, 1)
+        order = [2, far, n_row - far, 0]
+    else:
+        order = [*range(1, n_row), 0]
     across = []
     for side, part, step in ((0, 0, -1), (1, 2, 1)):
         for c in range(5):
@@ -198,15 +210,15 @@
                 preferred_element_type=jnp.float32,
             ).astype(csend.dtype)
             csend[side, :, c * slab:(c + 1) * slab] = piece
-        for k in order:
+        for turn, k in enumerate(order):
             t = pl.multiple_of(lax.rem(me_r + k, n_row) * rows, rows)
             copy = pltpu.make_async_remote_copy(
                 src_ref=csend.at[side, pl.ds(t, rows)], dst_ref=crecv.at[side, pl.ds(t, rows)],
-                send_sem=csend_sem.at[side, k], recv_sem=crecv_sem.at[side, k],
+                send_sem=csend_sem.at[side, turn], recv_sem=crecv_sem.at[side, turn],
                 device_id=device(0, step), device_id_type=MESH,
             )
             copy.start()
-            across.append((k, copy))
+            across.append((turn, copy))
     for c in range(5):
         own[:, c * slab:(c + 1) * slab] = jnp.dot(
             wt[slab:2 * slab, :], img[:, c * slab:(c + 1) * slab], preferred_element_type=jnp.float32
@@ -226,31 +238,62 @@
             parts.append(functools.reduce(jnp.add, terms))
         return parts
 
+    inner = (me_r > 0) & (me_r < n_row - 1)
     down = []
-    for k in order:
+    for turn, k in enumerate(order):
+        last = turn == n_row - 2
         for other, copy in across:
-            if other == k:
+            if other == turn:
                 copy.wait_recv()
         t = pl.multiple_of(lax.rem(me_r + k, n_row) * rows, rows)
+        if relayed and last:
+            @pl.when(inner)
+            def _():
+                down[0].wait_recv()
+
         for c, value in enumerate(combined(t)):
-            if k:
-                zsend[k, :, c * slab:(c + 1) * slab] = value.astype(zsend.dtype)
+            at = slice(c * slab, (c + 1) * slab)
+            if turn == n_row - 1:
+                out_ref[:, at] = value
+                continue
+            zsend[turn, :, at] = value.astype(zsend.dtype)
+            if relayed and last:
+                @pl.when(inner)
+                def _(value=value, at=at):
+                    zsend[turn, :, at] = (value + zrecv[2, :, at].astype(jnp.float32)).astype(zsend.dtype)
+        if turn == n_row - 1:
+            continue
+        steps = k
+        if relayed and turn == 0:
+            steps = jnp.where(inner, 2, jnp.where(me_r == 0, 1, n_row - 1))
+        copy = pltpu.make_async_remote_copy(
+            src_ref=zsend.at[turn], dst_ref=zrecv.at[k],
+            send_sem=zsend_sem.at[turn], recv_sem=zrecv_sem.at[k],
+            device_id=device(steps, 0), device_id_type=MESH,
+        )
+        copy.start()
+        down.append(copy)
+
+    def take(k):
+        out_ref[...] += zrecv[k].astype(jnp.float32)
+
+    if relayed:
+        for k, copy in enumerate(down):
+            if k == 0:
+                @pl.when(jnp.logical_not(inner))
+                def _():
+                    down[0].wait_recv()
+                    take(2)
             else:
-                out_ref[:, c * slab:(c + 1) * slab] = value
-        if k:
-            copy = pltpu.make_async_remote_copy(
-                src_ref=zsend.at[k], dst_ref=zrecv.at[k],
-                send_sem=zsend_sem.at[k], recv_sem=zrecv_sem.at[k],
-                device_id=device(k, 0), device_id_type=MESH,
-            )
-            copy.start()
-            down.append((k, copy))
-    for k, copy in down:
-        copy.wait_recv()
-        out_ref[...] += zrecv[k].astype(jnp.float32)
+                copy.wait_recv()
+                take(order[k])
+    else:
+        for turn, copy in enumerate(down):
+            copy.wait_recv()
+            take(order[turn])
     for copy in halo:
         copy.wait_send()
-    for _, copy in across + down:
+    for copy in [copy for _, copy in across] + down:
         copy.wait_send()
 
 
@@ -276,13 +319,16 @@
     bf, f32 = jnp.bfloat16, jnp.float32
     dma = pltpu.SemaphoreType.DMA
     vmem = pl.BlockSpec(memory_space=pltpu.VMEM)
+    hbm = pl.BlockSpec(memory_space=pltpu.HBM)
     smem = pl.BlockSpec(memory_space=pltpu.SMEM)
     out = pl.pallas_call(
         functools.partial(kernel, (fx, fy, ka, kp, b), n_row, n_col),
         out_shape=jax.ShapeDtypeStruct((rows, band), f32),
-        in_specs=[vmem, vmem, smem, smem, vmem],
+        in_specs=[hbm, hbm, smem, smem, vmem],
         out_specs=vmem,
         scratch_shapes=[
+            pltpu.VMEM((blocks * ka, b, b), bf),
+            pltpu.VMEM((blocks * kp, b, b), bf),
             pltpu.VMEM((fx + 2, fy + 2, b, kp * b), bf),
             pltpu.VMEM((9, *codes.shape), jnp.int32),
             pltpu.SMEM((9, *codes.shape), jnp.int32),
@@ -301,7 +347,7 @@
             pltpu.VMEM((slab, 5 * slab), f32),
             pltpu.VMEM((n_row, rows, band), bf),
             pltpu.VMEM((n_row, rows, band), bf),
-            dma((8,)), dma((8,)), dma((8,)), dma((8,)), dma,
+            dma((8,)), dma((8,)), dma((8,)), dma((8,)), dma, dma, dma,
             dma((2, n_row)), dma((2, n_row)), dma((n_row,)), dma((n_row,)),
         ],
         compiler_params=pltpu.CompilerParams(

time: 59.6 us -> 53.8 us (0.903)
  the two profiles are of different devices: /device:TPU:11 before, /device:TPU:0 now
where the time goes in v2:
time: 53.8 us; the launch traced here: 53.6 us
  Pallas kernels  48.6 us (90%)
  local copies, waits for them, and re-layouts  3.28 us (6%)
  other arithmetic  1.67 us (3%)
    pallas_call x1, Pallas kernels, per_device(): pl.pallas_call(functools.partial(kernel, (fx, fy, ka, kp, b), n_row, n_co...  48.6 us
    unnamed x4, local copies, waits for them, and re-layouts  2.98 us

profile of v2, /device:TPU:0, one launch (start us, length us, event | category | flops | bytes accessed | tf_op | source)
XLA Modules:
  0.0 53.6 jit_solution(8840358566431420213)
XLA Ops:
  0.0 0.7 %fusion.5 = s32[4,4,6]{2,1,0:T(4,128)S(1)} fusion(s32[4,4,6]{2,1,0:T(4,128)} %param.9, s32[]{:T(128)S(6)} %axis_index.12), kind=kLoop, calls=%fused_computation.18 | loop fusion | flops 3264 | bytes 772 | tf_op jit(solution)/shard_map/add | solution.py:314
  0.7 0.1 copy.7
  0.8 0.1 select_reduce_fusion.1
  0.9 0.1 reshape.25
  1.0 0.7 %iota_compare_fusion.2 = pred[4,4,9]{1,2,0:T(8,128)(4,1)S(1)} fusion(s32[4,4]{1,0:T(4,128)} %param.7), kind=kLoop, calls=%fused_computation.5 | loop fusion | flops 144 | bytes 208 | tf_op jit(solution)/shard_map/lt | solution.py:312
  1.7 0.8 %copy.6 = s32[4,4,9]{1,2,0:T(8,128)S(1)} copy(s32[4,4,9]{2,1,0:T(4,128)} %param.6) | data formatting | bytes 1152 | tf_op args[1]
  2.5 0.1 select_reduce_fusion
  2.7 0.1 reshape.24.ainv_ref
  2.8 0.0 copy-start
  2.8 1.4 %copy-done = bf16[4,4,6,64,64]{4,3,2,1,0:T(8,128)(2,1)S(1)} copy-done((bf16[4,4,6,64,64]{4,3,2,1,0:T(8,128)(2,1)S(1)}, bf16[4,4,6,64,64]{4,3,2,1,0:T(8,128)(2,1)}, u32[]{:S(2)}) %copy-start) | copy-done | bytes 786456
  4.2 48.6 %shard_map.55 = f32[64,1792]{1,0:T(8,128)S(1)} custom-call(bf16[144,64,64]{2,1,0:T(8,128)(2,1)} %bitcast.5, bf16[96,64,64]{2,1,0:T(8,128)(2,1)S(1)} %bitcast.4, s32[144]{0:T(256)S(1)} %reshape.24.ainv_ref, s32[8,128]{1,0:T(8,128)S(1)} %pad.4.codes_smem.codes_ref, s32[8,128]{1,0:T(8,128)S(1)} %pad.4.codes_smem.codes_ref), custom_call_target="tpu_custom_call" | custom-call | tf_op jit(solution)/shard_map/pallas_call | solution.py:324
  52.8 0.8 %copy.9 = f32[1,64,1792]{2,1,0:T(8,128)} copy(f32[1,64,1792]{2,1,0:T(8,128)S(1)} %bitcast.3) | data formatting | bytes 917504
  (1 shorter events, 0.0 us)
Async XLA Ops:
  2.8 1.4 %copy-start = (bf16[4,4,6,64,64]{4,3,2,1,0:T(8,128)(2,1)S(1)}, bf16[4,4,6,64,64]{4,3,2,1,0:T(8,128)(2,1)}, u32[]{:S(2)}) copy-start(bf16[4,4,6,64,64]{4,3,2,1,0:T(8,128)(2,1)} %param.8) | copy-start | bytes 2359300

commit v3 on v2

--- a/solution.py
+++ b/solution.py
@@ -13,7 +13,7 @@
 
 
 def kernel(
-    dims, n_row, n_col, a_hbm, p_hbm, ainv_ref, codes_smem, codes_ref, out_ref,
+    dims, n_row, n_col, a_hbm, p_hbm, ainv_ref, live_ref, codes_smem, codes_ref, out_ref,
     a_ref, p_ref, pext, cext, csm, p2, wc, wl, wr, wt, ac, al, ar, acc, img,
     csend, crecv, own, zsend, zrecv,
     psend_sem, precv_sem, ksend_sem, krecv_sem, copy_sem, a_sem, p_sem,
@@ -112,7 +112,8 @@
     def operator_tile(m, d):
         k = ainv_ref[m * 9 + d]
         tile = a_ref[m * ka + jnp.minimum(k, ka - 1)]
-        return jnp.where(jnp.full(tile.shape, k) < ka, tile, jnp.zeros_like(tile))
+        used = jnp.full(tile.shape, k) < jnp.full(tile.shape, live_ref[m // fy, m % fy])
+        return jnp.where(used, tile, jnp.zeros_like(tile))
 
     zero_tile = jnp.zeros((b, b), a_ref.dtype)
     operator_in.wait()
@@ -157,42 +158,59 @@
                 total = term if total is None else total + term
         acc[x, :, slab:4 * slab] = total
 
-    for copy in halo:
+    for copy in halo[::2]:
         copy.wait_recv()
     numbers_in = pltpu.make_async_copy(cext, csm, copy_sem)
     numbers_in.start()
     numbers_in.wait()
 
-    def edge_rows(y, carry):
-        at = pl.multiple_of(y * b, b)
-        spread(0, y + 1, (fx - 1) * fy + y, read_near(1), to_centre, (0, at))
-        spread(fx + 1, y + 1, y, read_near(7), to_centre, (fx + 1, at))
-        return carry
-
-    lax.fori_loop(0, fy, edge_rows, 0)
-
-    def edge_columns(x, carry):
+    def arrived(i, j):
+        halo[2 * around.index((-i, -j)) + 1].wait_recv()
+
+    def left_column(x, carry):
         at = pl.multiple_of((x + 1) * b, b)
         spread(x + 1, 0, x * fy + fy - 1, read_near(3), to_left, at)
+        return carry
+
+    def right_column(x, carry):
+        at = pl.multiple_of((x + 1) * b, b)
         spread(x + 1, fy + 1, x * fy, read_near(5), to_right, at)
         return carry
 
-    lax.fori_loop(0, fx, edge_columns, 0)
+    def top_row(y, carry):
+        spread(0, y + 1, (fx - 1) * fy + y, read_near(1), to_centre, (0, pl.multiple_of(y * b, b)))
+        return carry
+
+    def bottom_row(y, carry):
+        spread(fx + 1, y + 1, y, read_near(7), to_centre, (fx + 1, pl.multiple_of(y * b, b)))
+        return carry
+
+    arrived(0, -1)
+    lax.fori_loop(0, fx, left_column, 0)
+    arrived(0, 1)
+    lax.fori_loop(0, fx, right_column, 0)
+    arrived(-1, -1)
     spread(0, 0, fx * fy - 1, read_near(0), to_left, 0)
+    arrived(1, -1)
+    spread(fx + 1, 0, fy - 1, read_near(6), to_left, (fx + 1) * b)
+    left = jnp.dot(al[...], wl[...], preferred_element_type=jnp.float32)
+    for x in range(fx):
+        acc[x, 0:b, 0:3 * slab] += left[x * b:(x + 1) * b]
+    arrived(-1, 1)
     spread(0, fy + 1, (fx - 1) * fy, read_near(2), to_right, 0)
-    spread(fx + 1, 0, fy - 1, read_near(6), to_left, (fx + 1) * b)
+    arrived(1, 1)
     spread(fx + 1, fy + 1, 0, read_near(8), to_right, (fx + 1) * b)
-
+    right = jnp.dot(ar[...], wr[...], preferred_element_type=jnp.float32)
+    for x in range(fx):
+        acc[x, (fy - 1) * b:, 2 * slab:] += right[x * b:(x + 1) * b]
+    arrived(-1, 0)
+    lax.fori_loop(0, fy, top_row, 0)
     acc[0, :, slab:4 * slab] += jnp.dot(ac[0], wc[0], preferred_element_type=jnp.float32)
+    arrived(1, 0)
+    lax.fori_loop(0, fy, bottom_row, 0)
     acc[fx - 1, :, slab:4 * slab] += jnp.dot(
         ac[(fx - 1) * 3 + 2], wc[fx + 1], preferred_element_type=jnp.float32
     )
-    left = jnp.dot(al[...], wl[...], preferred_element_type=jnp.float32)
-    for x in range(fx):
-        acc[x, 0:b, 0:3 * slab] += left[x * b:(x + 1) * b]
-    right = jnp.dot(ar[...], wr[...], preferred_element_type=jnp.float32)
-    for x in range(fx):
-        acc[x, (fy - 1) * b:, 2 * slab:] += right[x * b:(x + 1) * b]
     for x in range(fx):
         img[x * fy * b:(x + 1) * fy * b, :] = acc[x].astype(img.dtype)
 
@@ -309,7 +327,7 @@
     band = 7 * slab
     blocks = fx * fy
     slots = jnp.arange(ka, dtype=jnp.int32)[:, None]
-    match = (neighbour_codes[..., None] == jnp.arange(9, dtype=jnp.int32)) & (slots < live_slots[..., None, None])
+    match = neighbour_codes[..., None] == jnp.arange(9, dtype=jnp.int32)
     ainv = jnp.min(jnp.where(match, slots, ka), axis=2).reshape(-1)
     place = jnp.mod(coarse_blocks // CB - slab_index + 1, n_col) * CB + coarse_blocks % CB
     tiles = jnp.arange(kp, dtype=jnp.int32)[:, None]
@@ -324,7 +342,7 @@
     out = pl.pallas_call(
         functools.partial(kernel, (fx, fy, ka, kp, b), n_row, n_col),
         out_shape=jax.ShapeDtypeStruct((rows, band), f32),
-        in_specs=[hbm, hbm, smem, smem, vmem],
+        in_specs=[hbm, hbm, smem, smem, smem, vmem],
         out_specs=vmem,
         scratch_shapes=[
             pltpu.VMEM((blocks * ka, b, b), bf),
@@ -354,7 +372,7 @@
             collective_id=0, has_side_effects=True, vmem_limit_bytes=50 * 1024 * 1024
         ),
     )(
-        operator_tiles.reshape(-1, b, b), prolong_tiles.reshape(-1, b, b), ainv, codes, codes,
+        operator_tiles.reshape(-1, b, b), prolong_tiles.reshape(-1, b, b), ainv, live_slots, codes, codes,
     )
     return out[None]
 

time: 53.8 us -> 54.3 us (level)
  other arithmetic: 1.67 us -> 0.94 us
  local copies, waits for them, and re-layouts: 3.28 us -> 3.96 us
    lt x1 -> x0, other arithmetic: 0.7 us -> none  [per_device(): slots < live_slots[..., None, None]]
    unnamed x4 -> x6, local copies, waits for them, and re-layouts: 2.98 us -> 3.66 us
where the time goes in v3:
time: 54.3 us; the launch traced here: 54 us
  Pallas kernels  49 us (90%)
  local copies, waits for them, and re-layouts  3.96 us (7%)
  other arithmetic  0.94 us (2%)
    pallas_call x1, Pallas kernels, per_device(): pl.pallas_call(functools.partial(kernel, (fx, fy, ka, kp, b), n_row, n_co...  49 us
    unnamed x6, local copies, waits for them, and re-layouts  3.66 us

profile of v3, /device:TPU:0, one launch (start us, length us, event | category | flops | bytes accessed | tf_op | source)
XLA Modules:
  0.0 54.0 jit_solution(12045202499261475456)
XLA Ops:
  0.0 0.7 %fusion.4 = s32[4,4,6]{2,1,0:T(4,128)S(1)} fusion(s32[4,4,6]{2,1,0:T(4,128)} %param.9, s32[]{:T(128)S(6)} %axis_index.12), kind=kLoop, calls=%fused_computation.16 | loop fusion | flops 3264 | bytes 772 | tf_op jit(solution)/shard_map/add | solution.py:332
  0.7 0.1 copy.7
  0.8 0.1 select_reduce_fusion.1
  0.9 0.1 reshape.17
  1.0 0.8 %copy.6 = s32[4,4,9]{1,2,0:T(8,128)S(1)} copy(s32[4,4,9]{2,1,0:T(4,128)} %param.6) | data formatting | bytes 1152 | tf_op args[1]
  1.9 0.1 select_reduce_fusion
  2.0 0.1 reshape.16.ainv_ref
  2.1 0.0 copy-start
  2.1 1.4 %copy-done = bf16[4,4,6,64,64]{4,3,2,1,0:T(8,128)(2,1)S(1)} copy-done((bf16[4,4,6,64,64]{4,3,2,1,0:T(8,128)(2,1)S(1)}, bf16[4,4,6,64,64]{4,3,2,1,0:T(8,128)(2,1)}, u32[]{:S(2)}) %copy-start) | copy-done | bytes 786456
  3.5 0.0 copy-start.1
  3.5 0.7 %copy-done.1 = s32[4,4]{1,0:T(4,128)S(1)} copy-done((s32[4,4]{1,0:T(4,128)S(1)}, s32[4,4]{1,0:T(4,128)}, u32[]{:S(2)}) %copy-start.1) | copy-done | bytes 88
  4.2 49.0 %shard_map.55 = f32[64,1792]{1,0:T(8,128)S(1)} custom-call(bf16[144,64,64]{2,1,0:T(8,128)(2,1)} %bitcast.5, bf16[96,64,64]{2,1,0:T(8,128)(2,1)S(1)} %bitcast.4, s32[144]{0:T(256)S(1)} %reshape.16.ainv_ref, s32[4,4]{1,0:T(4,128)S(1)} %copy-done.1, s32[8,128]{1,0:T(8,128)S(1)} %pad.4.codes_smem.codes_ref, s32[8,128]{1,0:T(8,128)S(1)} %pad.4.codes_smem.codes_ref), custom_call_target="tpu_custom_call" | custom-call | tf_op jit(solution)/shard_map/pallas_call | solution.py:342
  53.2 0.8 %copy.9 = f32[1,64,1792]{2,1,0:T(8,128)} copy(f32[1,64,1792]{2,1,0:T(8,128)S(1)} %bitcast.3) | data formatting | bytes 917504
  (1 shorter events, 0.0 us)
Async XLA Ops:
  2.1 1.4 %copy-start = (bf16[4,4,6,64,64]{4,3,2,1,0:T(8,128)(2,1)S(1)}, bf16[4,4,6,64,64]{4,3,2,1,0:T(8,128)(2,1)}, u32[]{:S(2)}) copy-start(bf16[4,4,6,64,64]{4,3,2,1,0:T(8,128)(2,1)} %param.8) | copy-start | bytes 2359300
  3.5 0.7 %copy-start.1 = (s32[4,4]{1,0:T(4,128)S(1)}, s32[4,4]{1,0:T(4,128)}, u32[]{:S(2)}) copy-start(s32[4,4]{1,0:T(4,128)} %live_ref.1) | copy-start | bytes 196

commit v4 on v2

--- a/solution.py
+++ b/solution.py
@@ -68,8 +68,10 @@
             device_id=device(i, j), device_id_type=MESH,
         )
         halo += [numbers, tiles]
-    for copy in halo:
+    for copy in halo[::2]:
         copy.start()
+    for t in sorted(range(len(around)), key=lambda t: (around[t][0] == 0, around[t][1] != 0)):
+        halo[2 * t + 1].start()
 
     lane = lax.broadcasted_iota(jnp.int32, (b, 2 * b), 1)
     lower = lane < b
@@ -351,7 +353,7 @@
             dma((2, n_row)), dma((2, n_row)), dma((n_row,)), dma((n_row,)),
         ],
         compiler_params=pltpu.CompilerParams(
-            collective_id=0, has_side_effects=True, vmem_limit_bytes=50 * 1024 * 1024
+            collective_id=0, has_side_effects=True, vmem_limit_bytes=60 * 1024 * 1024
         ),
     )(
         operator_tiles.reshape(-1, b, b), prolong_tiles.reshape(-1, b, b), ainv, codes, codes,

time: 53.8 us -> 56 us (1.041)
  Pallas kernels: 48.6 us -> 49.6 us
  local copies, waits for them, and re-layouts: 3.28 us -> 4.1 us
    pallas_call x1, Pallas kernels: 48.6 us -> 49.6 us  [per_device(): pl.pallas_call(functools.partial(kernel, (fx, fy, ka, kp, b), n_row, n_co...]
    pad x1, local copies, waits for them, and re-layouts: 0.01 us -> 0.61 us  [per_device(): codes = jnp.pad(pinv, ((0, -pinv.shape[0] % 8), (0, 0)))]
    reshape x1, local copies, waits for them, and re-layouts: 0.09 us -> 0.68 us  [per_device(): ainv = jnp.min(jnp.where(match, slots, ka), axis=2).reshape(-1)]
    unnamed x4 -> x2, local copies, waits for them, and re-layouts: 2.98 us -> 2.62 us
where the time goes in v4:
time: 56 us; the launch traced here: 55.4 us
  Pallas kernels  49.6 us (89%)
  local copies, waits for them, and re-layouts  4.1 us (7%)
  other arithmetic  1.67 us (3%)
    pallas_call x1, Pallas kernels, per_device(): pl.pallas_call(functools.partial(kernel, (fx, fy, ka, kp, b), n_row, n_co...  49.6 us
    unnamed x2, local copies, waits for them, and re-layouts  2.62 us

profile of v4, /device:TPU:0, one launch (start us, length us, event | category | flops | bytes accessed | tf_op | source)
XLA Modules:
  0.0 55.4 jit_solution(941102185091277832)
XLA Ops:
  0.0 0.7 %fusion.5 = s32[4,4,6]{2,1,0:T(4,128)S(1)} fusion(s32[4,4,6]{2,1,0:T(4,128)} %param.9, s32[]{:T(128)S(6)} %axis_index.12), kind=kLoop, calls=%fused_computation.18 | loop fusion | flops 3264 | bytes 772 | tf_op jit(solution)/shard_map/add | solution.py:316
  0.7 0.1 copy.7
  0.8 0.1 select_reduce_fusion.1
  0.9 0.1 reshape.25
  1.0 0.6 %pad.4.codes_smem.codes_ref = s32[8,128]{1,0:T(8,128)} pad(s32[2,128]{1,0:T(2,128)S(1)} %reshape.25, s32[]{:T(128)} %constant.43.clone.1), padding=0_6x0_0 | pad | bytes 5124 | tf_op jit(solution)/shard_map/jit(_pad)/pad | solution.py:320
  1.6 0.7 %iota_compare_fusion.2 = pred[4,4,9]{1,2,0:T(8,128)(4,1)S(1)} fusion(s32[4,4]{1,0:T(4,128)} %param.7), kind=kLoop, calls=%fused_computation.5 | loop fusion | flops 144 | bytes 208 | tf_op jit(solution)/shard_map/lt | solution.py:314
  2.3 0.8 %copy.6 = s32[4,4,9]{1,2,0:T(8,128)S(1)} copy(s32[4,4,9]{2,1,0:T(4,128)} %param.6) | data formatting | bytes 1152 | tf_op args[1]
  3.1 0.1 select_reduce_fusion
  3.3 0.7 %reshape.24.ainv_ref = s32[144]{0:T(256)} reshape(s32[4,4,9]{2,1,0:T(4,128)S(1)} %select_reduce_fusion) | data formatting | bytes 1152 | tf_op jit(solution)/shard_map/reshape | solution.py:315
  4.0 49.6 %shard_map.55 = f32[64,1792]{1,0:T(8,128)} custom-call(bf16[144,64,64]{2,1,0:T(8,128)(2,1)} %bitcast.3, bf16[96,64,64]{2,1,0:T(8,128)(2,1)} %bitcast.5, s32[144]{0:T(256)} %reshape.24.ainv_ref, s32[8,128]{1,0:T(8,128)} %pad.4.codes_smem.codes_ref, s32[8,128]{1,0:T(8,128)} %pad.4.codes_smem.codes_ref), custom_call_target="tpu_custom_call" | custom-call | tf_op jit(solution)/shard_map/pallas_call | solution.py:326
  53.6 1.8 %copy.9 = f32[1,64,1792]{2,1,0:T(8,128)} copy(f32[1,64,1792]{2,1,0:T(8,128)} %bitcast.4) | data formatting | bytes 917504
